TPU v7x, 32 devices: a whole 2x2x4 slice. The times are simulated.
32 devices in a mesh: row: 8 (over z, core), col: 4 (over y, x).
Axes of the slice: x: 2, y: 2, z: 4, core: 2. Of those that a mesh axis runs over, the one named last changes fastest.
Arguments:
- f_blocks: bfloat16 [16384, 2048], P('row', 'col'), may hold values from -0.25 to 0.25
- block_cols: int32 [256, 32], P('row', 'col'), may hold values from 0 to 23, as said below
- block_counts: int32 [256, 4], P('row', 'col'), may hold values from 1 to 8, as said below
- p_matrix: bfloat16 [12288, 2048], P('row', 'col'), may hold values from -6 to 6
Outputs:
- product: bfloat16 [16384, 2048], P('row', 'col')
Inputs may be any that keep to these rules, and one draw needn't show every extreme that they name: `block_cols`: within one block row of one stored tile the 8 listed block columns are distinct, padded slots included. `block_counts`: some block row of every stored tile is full.
All inputs are finite; a program needn't handle non-finite values.
Results may differ from a plain program's by a relative error of at most 0.001.
Values may be sent and summed in bfloat16 or wider, within the bound.
No kernel may reach another device: no remote copies, remote signals or barrier semaphores. Data moves between devices by JAX's collectives and lax.ppermute only.
A program may use at most 64 MiB of HBM per device.

v0:
```python
import functools

import jax
import jax.numpy as jnp
from jax import lax
from jax.experimental import pallas as pl
from jax.experimental.pallas import tpu as pltpu
from jax.sharding import PartitionSpec as P

GROUP = 4
PAIR = 2

SMEM = pl.BlockSpec(memory_space=pltpu.SMEM)
ANY = pl.BlockSpec(memory_space=pl.ANY)
HBM = pl.BlockSpec(memory_space=pltpu.HBM)


def shifted(block, axis, distance):
    devices = range(lax.axis_size(axis))
    route = [((i - distance) % len(devices), i) for i in devices]
    return lax.ppermute(block, axis, route)


def in_hbm(x):
    return pltpu.with_memory_space_constraint(x, pltpu.HBM)


def params(mib):
    return pltpu.CompilerParams(vmem_limit_bytes=mib << 20)


def cost(flops, moved):
    return pl.CostEstimate(flops=flops, bytes_accessed=moved, transcendentals=0)


def piece(edge, index, count=1):
    return pl.ds(pl.multiple_of(index * edge, edge), count * edge)


def beyond(count):
    more = jnp.maximum(count - PAIR, 0)
    return more // PAIR, more % PAIR


def walk(counts, full_at, single_at, row_done):
    at, opened = jnp.int32(0), jnp.int32(-1)
    for r in range(len(counts)):
        full, single = beyond(counts[r])
        full_at(r, at)
        shares = jnp.logical_and(single == 1, opened >= 0)
        opens = jnp.logical_and(single == 1, opened < 0)
        single_at(r, jnp.where(shares, opened, at + full), shares)
        opened = jnp.where(opens, at + full, jnp.where(shares, -1, opened))
        at = at + full + opens.astype(jnp.int32)
        row_done(r, at, opened)


def write_table(notes, slots, table):
    nrows = notes.shape[1]

    def full_at(r, at):
        table[0, r] = at

    def single_at(r, at, shares):
        table[1, r] = at * 2 + shares.astype(jnp.int32)

    def row_done(r, at, opened):
        table[0, r + 1] = at
        table[2, r + 1] = jnp.where(opened < 0, at, opened)

    table[2, 0] = jnp.int32(0)
    walk([notes[slots, r] for r in range(nrows)], full_at, single_at, row_done)


def table_shape(nrows):
    return jax.ShapeDtypeStruct((3, nrows + 1), jnp.int32)


def read_kernel(slots, notes, notes_next, table, most_ref):
    write_table(notes_next, slots, table)
    nrows = notes.shape[1]
    full, single = jnp.int32(0), jnp.int32(0)
    for r in range(nrows):
        more, rest = beyond(notes[slots, r])
        full, single = full + more, single + rest
    most = jnp.maximum(full + (single + 1) // PAIR, table[0, nrows])
    most_ref[...] = jnp.full(most_ref.shape, most, jnp.int32)


def read_notes(notes, notes_next, slots):
    return pl.pallas_call(
        functools.partial(read_kernel, slots),
        in_specs=[SMEM, SMEM],
        out_specs=[SMEM, pl.BlockSpec(memory_space=pltpu.VMEM)],
        out_shape=[table_shape(notes.shape[1]), jax.ShapeDtypeStruct((8, 128), jnp.int32)],
        cost_estimate=cost(20 << 30, 4096),
        compiler_params=params(2),
        name="read_notes",
    )(notes, notes_next)


def pick_kernel(ends, one_ref, other_ref, size):
    most = jnp.max(jnp.maximum(one_ref[...], other_ref[...]))
    index = jnp.int32(0)
    for end in ends[:-1]:
        index = index + (most > end).astype(jnp.int32)
    size[0] = index


def pick_size(ends, one, other):
    vector = pl.BlockSpec(memory_space=pltpu.VMEM)
    return pl.pallas_call(
        functools.partial(pick_kernel, ends),
        in_specs=[vector, vector],
        out_specs=SMEM,
        out_shape=jax.ShapeDtypeStruct((1,), jnp.int32),
        cost_estimate=cost(0, 4096),
        compiler_params=params(2),
        name="pick_size",
    )(one, other)


def leading_kernel(f_ref, cols_ref, counts_ref, out_ref):
    slots, nrows = cols_ref.shape
    tall = f_ref.shape[0]
    out_ref[pl.ds(0, tall), :] = f_ref[...]
    notes = jnp.concatenate([cols_ref[...], jnp.broadcast_to(counts_ref[...], (slots, nrows))], axis=0)
    out_ref[pl.ds(tall, 2 * slots), pl.ds(0, nrows)] = notes.astype(jnp.float32).astype(out_ref.dtype)


def leading_pieces(rows, f_blocks, cols, counts):
    slots, nrows = cols.shape
    edge = f_blocks.shape[0] // nrows
    shape = (rows * edge + 2 * slots, PAIR * edge)
    f_blocks, cols, counts = (in_hbm(x) for x in (f_blocks, cols, counts))
    return pl.pallas_call(
        leading_kernel,
        grid=(1,),
        in_specs=[
            pl.BlockSpec((rows * edge, PAIR * edge), lambda g: (0, 0)),
            pl.BlockSpec(cols.shape, lambda g: (0, 0)),
            pl.BlockSpec(counts.shape, lambda g: (0, 0)),
        ],
        out_specs=pl.BlockSpec(shape, lambda g: (0, 0)),
        out_shape=jax.ShapeDtypeStruct(shape, f_blocks.dtype),
        cost_estimate=cost(0, 4 * rows * edge * PAIR * edge),
        compiler_params=params(8),
        name="leading_pieces",
    )(f_blocks, cols, counts)


def pack_kernel(edge, slots, notes, f_ref, out_ref, extra_ref, table, f_here, packed, sems):
    nrows = notes.shape[1]
    parts = slots // PAIR
    fetched = []
    for g in range(nrows // GROUP):
        here = piece(edge, g * GROUP, GROUP)
        fetched.append(pltpu.make_async_copy(f_ref.at[here], f_here.at[here], sems.at[g]))
        fetched[-1].start()
    wide = PAIR * edge

    def strip(r, p):
        return f_here[pl.ds(r * edge, edge), pl.ds(pl.multiple_of(p * wide, wide), wide)]

    def full_at(r, at):
        if r % GROUP == 0:
            fetched[r // GROUP].wait()
        packed[pl.ds(r * edge, edge), :] = strip(r, 0)
        for p in range(1, parts):
            packed[piece(edge, nrows + at + (p - 1)), :] = strip(r, p)

    def single_at(r, at, shares):
        @pl.when(shares)
        def _():
            value = strip(r, 1 + beyond(notes[slots, r])[0])
            here = piece(edge, nrows + at)
            moved = jnp.concatenate([value[:, edge:], value[:, :edge]], axis=1)
            low = lax.broadcasted_iota(jnp.int32, value.shape, 1) < edge
            packed[here, :] = jnp.where(low, packed[here, :], moved)

    walk([notes[slots, r] for r in range(nrows)], full_at, single_at, lambda *_: None)
    copies = [
        pltpu.make_async_copy(packed.at[pl.ds(nrows * edge, extra_ref.shape[0])], extra_ref, sems.at[0]),
        pltpu.make_async_copy(packed, out_ref, sems.at[1]),
    ]
    for copy in copies:
        copy.start()
    write_table(notes, slots, table)
    for copy in copies:
        copy.wait()


def packed_pieces(notes, slots, always, f_blocks):
    nrows = notes.shape[1]
    edge = f_blocks.shape[0] // nrows
    shape = (nrows * slots // PAIR * edge, PAIR * edge)
    return pl.pallas_call(
        functools.partial(pack_kernel, edge, slots),
        in_specs=[SMEM, ANY],
        out_specs=[ANY, ANY, SMEM],
        scratch_shapes=[
            pltpu.VMEM(f_blocks.shape, f_blocks.dtype),
            pltpu.VMEM(shape, f_blocks.dtype),
            pltpu.SemaphoreType.DMA((nrows // GROUP,)),
        ],
        out_shape=[
            jax.ShapeDtypeStruct(shape, f_blocks.dtype),
            jax.ShapeDtypeStruct((always * edge, PAIR * edge), f_blocks.dtype),
            table_shape(nrows),
        ],
        cost_estimate=cost(0, 4 * f_blocks.size),
        compiler_params=params(16),
        name="pack_live_pieces",
    )(notes, f_blocks)


def cut_kernel(ranges, packed_ref, *refs):
    out_refs, sems = refs[: len(ranges)], refs[-1]
    copies = [
        pltpu.make_async_copy(packed_ref.at[pl.ds(low, high - low)], out_ref, sems.at[k])
        for k, ((low, high), out_ref) in enumerate(zip(ranges, out_refs))
    ]
    for copy in copies:
        copy.start()
    for copy in copies:
        copy.wait()


def cut_pieces(ranges, packed):
    edge = packed.shape[1] // PAIR
    rows = [(low * edge, high * edge) for low, high in ranges]
    return pl.pallas_call(
        functools.partial(cut_kernel, rows),
        in_specs=[ANY],
        out_specs=[ANY] * (2 * len(rows)),
        scratch_shapes=[pltpu.SemaphoreType.DMA((len(rows),))],
        out_shape=[jax.ShapeDtypeStruct((high - low, packed.shape[1]), packed.dtype) for low, high in rows] * 2,
        cost_estimate=cost(0, 4 * sum(high - low for low, high in rows) * packed.shape[1]),
        compiler_params=params(2),
        name="cut_pieces",
    )(packed)


def row_product(notes, table, slots, edge, row, held, p_ref):
    nrows = notes.shape[1]
    zero = p_ref.shape[0] // edge - 1
    count = notes[slots, row]
    full, single = beyond(count)
    code = table[1, row]
    second = code % 2
    left = [held[piece(edge, row), :]]
    picks = [notes[0, row], jnp.where(count > 1, notes[1, row], zero)]
    for p in range(slots // PAIR - 1):
        alone = jnp.logical_and(p == full, single == 1)
        at = jnp.where(p < full, nrows + table[0, row] + p, jnp.where(alone, nrows + code // 2, row))
        left.append(held[piece(edge, at), :])
        even, odd = notes[PAIR * (p + 1), row], notes[PAIR * (p + 1) + 1, row]
        picks.append(jnp.where(jnp.logical_or(p < full, jnp.logical_and(alone, second == 0)), even, zero))
        picks.append(jnp.where(p < full, odd, jnp.where(jnp.logical_and(alone, second == 1), even, zero)))
    picked = [p_ref[piece(edge, pick), :] for pick in picks]
    return jnp.dot(
        jnp.concatenate(left, axis=1), jnp.concatenate(picked, axis=0), preferred_element_type=jnp.float32
    )


def step_kernel(edge, slots, name, leading, places, notes, table, *refs):
    size = None
    if name == "late":
        size, *refs = refs
    part_refs, refs = refs[: len(places)], refs[len(places) :]
    p_ref, *refs = refs
    total_ref = None
    if name != "first":
        total_ref, *refs = refs
    if name == "late":
        _, *refs = refs
    out_ref, held, p_here, stage, sems, out_sems, *refs = refs
    nrows = notes.shape[1]
    groups = nrows // GROUP

    depth = p_ref.shape[0]
    p_copy = pltpu.make_async_copy(p_ref, p_here.at[pl.ds(0, depth)], sems.at[0])
    p_copy.start()
    p_here[pl.ds(depth, edge), :] = jnp.zeros((edge, p_here.shape[1]), p_here.dtype)

    low, high = 0, groups
    if name != "first":
        room = [count for kind, _, count in places if kind == "second"][0]
        done = jnp.int32(0)
        for g in range(leading // GROUP):
            done = done + (table[0, (g + 1) * GROUP] <= room).astype(jnp.int32)
        low, high = (0, done) if name == "early" else (done, groups)

    copies = []
    for (kind, at, count), part in zip(places, part_refs):
        step = count
        if name == "late" and kind == "second":
            step = -(-count // 4)
        for first in range(0, count, step):
            needed = None
            if name == "late" and kind == "first":
                needed = low < leading // GROUP
            elif name == "late" and kind == "second":
                needed = table[2, low * GROUP] < first + step
            elif not isinstance(kind, str):
                needed = size[0] == kind
            tall = min(step, count - first) * edge
            source = part.at[pl.ds(first * edge, tall)]
            target = held.at[pl.ds((at + first) * edge, tall)]
            copies.append((needed, pltpu.make_async_copy(source, target, sems.at[1 + len(copies)])))

    def each(act):
        for needed, copy in copies:
            if needed is None:
                act(copy)
            else:
                pl.when(needed)(functools.partial(act, copy))

    each(lambda copy: copy.start())

    def total_copy(g):
        here = piece(edge, g * GROUP, GROUP)
        return pltpu.make_async_copy(total_ref.at[here], refs[0].at[here], refs[1].at[g])

    def out_copy(g):
        here = piece(edge, g * GROUP, GROUP)
        return pltpu.make_async_copy(stage.at[here], out_ref.at[here], out_sems.at[g])

    def over(act):
        def step(g, carry):
            act(g)
            return carry

        lax.fori_loop(low, high, step, 0)

    if name != "first":
        over(lambda g: total_copy(g).start())
    each(lambda copy: copy.wait())
    p_copy.wait()

    def group(g):
        if name != "first":
            total_copy(g).wait()
        for r in range(GROUP):
            row = g * GROUP + r
            here = piece(edge, row)
            value = row_product(notes, table, slots, edge, row, held, p_here)
            if name != "first":
                value = refs[0][here, :] + value
            stage[here, :] = value.astype(stage.dtype)
        out_copy(g).start()

    over(group)
    over(lambda g: out_copy(g).wait())


def step_product(name, notes, table, slots, leading, places, parts, p_tile, total=None, size=None, out=None):
    nrows = notes.shape[1]
    depth, width = p_tile.shape
    edge = parts[0].shape[1] // PAIR
    groups = nrows // GROUP
    room = max(at + rows for _, at, rows in places)
    dtype = jnp.float32 if name == "first" else jnp.bfloat16
    tall = nrows * edge
    later = name != "first"
    late = name == "late"
    return pl.pallas_call(
        functools.partial(step_kernel, edge, slots, name, leading, places),
        in_specs=[SMEM] * (2 + late) + [ANY] * (len(parts) + 1 + later) + [HBM] * late,
        out_specs=HBM if later else ANY,
        scratch_shapes=[
            pltpu.VMEM((room * edge, PAIR * edge), p_tile.dtype),
            pltpu.VMEM((depth + edge, width), p_tile.dtype),
            pltpu.VMEM((tall, width), dtype),
            pltpu.SemaphoreType.DMA((len(parts) + 8,)),
            pltpu.SemaphoreType.DMA((groups,)),
        ]
        + [pltpu.VMEM((tall, width), jnp.float32), pltpu.SemaphoreType.DMA((groups,))] * later,
        out_shape=(pltpu.HBM if later else jax.ShapeDtypeStruct)((tall, width), dtype),
        input_output_aliases={5 + len(parts): 0} if late else {},
        cost_estimate=cost(tall * width * slots * edge, 4 * tall * width),
        compiler_params=params(16),
        name="step_" + name,
    )(
        notes,
        table,
        *([size] if late else []),
        *parts,
        p_tile,
        *([total] if later else []),
        *([in_hbm(out)] if late else []),
    )


def remainder(k, slots, leading, places, rests, unused, notes, table, lead, extra, p_second, total):
    rest = [shifted(part, "col", -1) if k == n else other for n, (part, other) in enumerate(zip(rests, unused))]
    return step_product("early", notes, table, slots, leading, places, (lead, extra), p_second, total), rest


def body(f_blocks, block_cols, block_counts, p_matrix):
    nrows, slots = block_cols.shape
    edge = f_blocks.shape[0] // nrows
    cols, counts = block_cols.T, block_counts.T
    groups = nrows // GROUP
    leading = (groups - groups // 4) * GROUP
    others = nrows * (slots // PAIR - 1)
    unit = others // 24
    always = 10 * unit
    ends = [always + k * unit for k in (1, 2, 3, 4, 5, 6, 8)] + [others]

    lead = shifted(leading_pieces(leading, f_blocks, cols, counts), "col", -1)
    notes = jnp.concatenate([cols, jnp.broadcast_to(counts, (slots, nrows))], axis=0)
    packed, extra, table = packed_pieces(notes, slots, always, f_blocks)
    p_second, packed = lax.optimization_barrier((p_matrix, packed))
    p_second = shifted(p_second, "row", -1)
    rests = cut_pieces([(nrows + always, nrows + end) for end in ends] + [(leading, nrows)], packed)
    rests, later, unused = rests[: len(ends)], rests[len(ends)], rests[len(ends) + 1 : -1]
    extra, *rests = lax.optimization_barrier((extra, *rests))
    extra = shifted(extra, "col", -1)
    every = packed.shape[0] // edge
    total = step_product("first", notes, table, slots, leading, [("all", 0, every)], (packed,), p_matrix)
    later, total, lead = lax.optimization_barrier((later, total, lead))
    later = shifted(later, "col", -1)

    notes_next = lead[leading * edge :, :nrows].astype(jnp.float32).astype(jnp.int32)
    table_next, most = read_notes(notes, notes_next, slots)
    other = most
    distance = 2
    while distance < lax.axis_size("col"):
        most = jnp.maximum(most, other)
        other = shifted(most, "col", -distance)
        distance *= 2
    size = pick_size(ends, most, other)
    early = [("first", 0, leading), ("second", nrows, always)]
    late = [early[0], ("later", leading, nrows - leading), early[1]]
    late += [(k, nrows + always, end - always) for k, end in enumerate(ends)]
    branches = [functools.partial(remainder, k, slots, leading, early) for k in range(len(ends))]
    out, rest = lax.switch(size[0], branches, rests, unused, notes_next, table_next, lead, extra, p_second, total)
    parts = (lead, later, extra, *rest)
    return step_product("late", notes_next, table_next, slots, leading, late, parts, p_second, total, size, out)


def solution(mesh):
    return jax.shard_map(
        body,
        mesh=mesh,
        in_specs=(P("row", "col"), P("row", "col"), P("row", "col"), P("row", "col")),
        out_specs=P("row", "col"),
        check_vma=False,
    )
```

profile of v0, /device:TPU:0, one launch (start us, length us, event | category | flops | bytes accessed | tf_op | source)
XLA Modules:
  0.0 42.6 jit_solution(1126901624226401213)
XLA Ops:
  0.0 1.2 %leading_pieces.1 = bf16[1552,128]{1,0:T(8,128)(2,1)S(1)} custom-call(bf16[2048,512]{1,0:T(8,128)(2,1)} %f_ref.3, s32[8,32]{1,0:T(8,128)} %bitcast.4, s32[1,32]{1,0:T(1,128)} %bitcast.6), custom_call_target="tpu_custom_call" | custom-call | bytes 786432 | tf_op jit(solution)/shard_map/leading_pieces/pallas_call | solution.py:136
  1.2 4.0 %collective-permute-start.8 = (bf16[1552,128]{1,0:T(8,128)(2,1)S(1)}, bf16[1552,128]{1,0:T(8,128)(2,1)S(1)}, u32[]{:S(2)}, u32[]{:S(2)}) collective-permute-start(bf16[1552,128]{1,0:T(8,128)(2,1)S(1)} %leading_pieces.1), channel_id=1, source_target_pairs={{1,0},{2,1},{3,2},{0,3},{5,4},{6,5},{7,6},{4,7},{9,8},{10,9},{11,1... | collective-permute-start | bytes 1191944 | tf_op jit(solution)/shard_map/ppermute | solution.py:21
  5.2 0.0 copy-done.4
  5.2 0.0 copy-done.3
  5.2 0.0 copy-done
  5.2 3.1 %pack_live_pieces.1 = (bf16[8192,128]{1,0:T(8,128)(2,1)S(1)}, bf16[2560,128]{1,0:T(8,128)(2,1)S(1)}, s32[3,33]{1,0:T(4,128)S(1)}) custom-call(s32[16,32]{1,0:T(8,128)S(1)} %pad_add_fusion.notes, bf16[2048,512]{1,0:T(8,128)(2,1)S(1)} %copy-done), custom_call_target="tpu_custom_call" | custom-call | bytes 4194304 | tf_op jit(solution)/shard_map/pack_live_pieces/pallas_call | solution.py:197
  8.3 2.9 %collective-permute-start.12 = (bf16[1536,512]{1,0:T(8,128)(2,1)S(1)}, bf16[1536,512]{1,0:T(8,128)(2,1)S(1)}, u32[]{:S(2)}, u32[]{:S(2)}) collective-permute-start(bf16[1536,512]{1,0:T(8,128)(2,1)S(1)} %copy-done.1), channel_id=1, source_target_pairs={{4,0},{8,4},{12,8},{16,12},{20,16},{24,20},{28,24},{0,28},{5,1},{9... | collective-permute-start | bytes 4718600 | tf_op jit(solution)/shard_map/ppermute | solution.py:21
  11.2 1.5 %cut_pieces.1 = (bf16[256,128]{1,0:T(8,128)(2,1)S(1)}, bf16[512,128]{1,0:T(8,128)(2,1)S(1)}, bf16[768,128]{1,0:T(8,128)(2,1)S(1)}, bf16[1024,128]{1,0:T(8,128)(2...) custom-call(bf16[8192,128]{1,0:T(8,128)(2,1)S(1)} %get-tuple-element, ...), custom_call_target="tpu_custom_call" | custom-call | bytes 5898240 | tf_op jit(solution)/shard_map/cut_pieces/pallas_call | solution.py:232
  12.7 0.9 %collective-permute-start.11 = (bf16[2560,128]{1,0:T(8,128)(2,1)S(1)}, bf16[2560,128]{1,0:T(8,128)(2,1)S(1)}, u32[]{:S(2)}, u32[]{:S(2)}) collective-permute-start(bf16[2560,128]{1,0:T(8,128)(2,1)S(1)} %get-tuple-element.403), channel_id=1, source_target_pairs={{1,0},{2,1},{3,2},{0,3},{5,4},{6,5},{7,6},{4,7},{9,8},{10,9},{11,1... | collective-permute-start | bytes 1966088 | tf_op jit(solution)/shard_map/ppermute | solution.py:21
  13.6 5.3 %step_first.1.refs_13_ = f32[2048,512]{1,0:T(8,128)S(1)} custom-call(s32[16,32]{1,0:T(8,128)S(1)} %pad_add_fusion.notes, s32[3,33]{1,0:T(4,128)S(1)} %get-tuple-element.389.table, bf16[8192,128]{1,0:T(8,128)(2,1)S(1)} %get-tuple-element.387.packed_ref.refs_0_, bf16[1536,512]{1,0:T(8,128)(2,1)S(1)} %copy-done.1), custom_call_target="tpu_custom_call" | custom-call | flops 536870912 | bytes 4194304 | tf_op jit(solution)/shard_map/step_first/pallas_call | solution.py:367
  18.9 0.0 collective-permute-done.8.refs_1_
  18.9 1.3 %collective-permute-start.10 = (bf16[512,128]{1,0:T(8,128)(2,1)S(1)}, bf16[512,128]{1,0:T(8,128)(2,1)S(1)}, u32[]{:S(2)}, u32[]{:S(2)}) collective-permute-start(bf16[512,128]{1,0:T(8,128)(2,1)S(1)} %get-tuple-element.393), channel_id=1, source_target_pairs={{1,0},{2,1},{3,2},{0,3},{5,4},{6,5},{7,6},{4,7},{9,8},{10,9},{11,1... | collective-permute-start | bytes 393224 | tf_op jit(solution)/shard_map/ppermute | solution.py:21
  20.2 1.8 %read_notes.1 = (s32[3,33]{1,0:T(4,128)S(1)}, s32[8,128]{1,0:T(8,128)S(1)}) custom-call(s32[16,32]{1,0:T(8,128)S(1)} %pad_add_fusion.notes, s32[16,32]{1,0:T(8,128)S(1)} %convert_convert_fusion.notes_next.notes), custom_call_target="tpu_custom_call" | custom-call | flops 21474836480 | bytes 4096 | tf_op jit(solution)/shard_map/read_notes/pallas_call | solution.py:91
  22.0 1.5 %collective-permute-start.9 = (s32[8,128]{1,0:T(8,128)S(1)}, s32[8,128]{1,0:T(8,128)S(1)}, u32[]{:S(2)}, u32[]{:S(2)}) collective-permute-start(s32[8,128]{1,0:T(8,128)S(1)} %get-tuple-element.392.one_ref), channel_id=1, source_target_pairs={{2,0},{3,1},{0,2},{1,3},{6,4},{7,5},{4,6},{5,7},{10,8},{11,9},{8,1... | collective-permute-start | bytes 12296 | tf_op jit(solution)/shard_map/ppermute | solution.py:21
  23.5 2.2 %collective-permute-done.9.other_ref = s32[8,128]{1,0:T(8,128)S(1)} collective-permute-done((s32[8,128]{1,0:T(8,128)S(1)}, s32[8,128]{1,0:T(8,128)S(1)}, u32[]{:S(2)}, u32[]{:S(2)}) %collective-permute-start.9) | collective-permute-done | bytes 4128 | tf_op jit(solution)/shard_map/ppermute | solution.py:21
  25.7 0.7 %pick_size.1.refs_0_ = s32[1]{0:T(128)} custom-call(s32[8,128]{1,0:T(8,128)S(1)} %get-tuple-element.392.one_ref, s32[8,128]{1,0:T(8,128)S(1)} %collective-permute-done.9.other_ref), custom_call_target="tpu_custom_call" | custom-call | bytes 4096 | tf_op jit(solution)/shard_map/pick_size/pallas_call | solution.py:112
  27.0 1.8 %collective-permute-done.11.refs_3_ = bf16[2560,128]{1,0:T(8,128)(2,1)S(1)} collective-permute-done((bf16[2560,128]{1,0:T(8,128)(2,1)S(1)}, bf16[2560,128]{1,0:T(8,128)(2,1)S(1)}, u32[]{:S(2)}, u32[]{:S(2)}) %collective-permute-start.11) | collective-permute-done | bytes 655392 | tf_op jit(solution)/shard_map/ppermute | solution.py:21
  28.9 0.2 collective-permute-done.12.refs_12_
  29.1 8.5 %conditional.1 = (bf16[2048,512]{1,0:T(8,128)(2,1)}, bf16[256,128]{1,0:T(8,128)(2,1)S(1)}, bf16[512,128]{1,0:T(8,128)(2,1)}, bf16[768,128]{1,0:T(8,128)(2,1)}, b...) conditional(s32[]{:T(128)} %bitcast.3, ...), branch_computations={%region_0.0_spmd, %region_1.0_spmd, %region_2.0_spmd, %region_3.0_... | conditional | flops 536870912 | bytes 7995504 | solution.py:438
  29.1 3.2 %collective-permute-start.3 = (bf16[1024,128]{1,0:T(8,128)(2,1)S(1)}, bf16[1024,128]{1,0:T(8,128)(2,1)}, u32[]{:S(2)}, u32[]{:S(2)}) collective-permute-start(bf16[1024,128]{1,0:T(8,128)(2,1)S(1)} %get-tuple-element.280), channel_id=1, source_target_pairs={{1,0},{2,1},{3,2},{0,3},{5,4},{6,5},{7,6},{4,7},{9,8},{10,9},{11,1... | collective-permute-start | bytes 786440 | tf_op jit(solution)/shard_map/cond/branch_3_fun/ppermute | solution.py:21
  32.3 5.3 %step_early.11 = bf16[2048,512]{1,0:T(8,128)(2,1)} custom-call(s32[16,32]{1,0:T(8,128)S(1)} %get-tuple-element.271.notes, s32[3,33]{1,0:T(4,128)S(1)} %get-tuple-element.272.table, bf16[1552,128]{1,0:T(8,128)(2,1)S(1)} %get-tuple-element.273.refs_0_, bf16[2560,128]{1,0:T(8,128)(2,1)S(1)} %get-tuple-element.274.refs_1_, ...), custom_call_target="tpu_custom_call" | custom-call | flops 536870912 | bytes 4194304 | tf_op jit(solution)/shard_map/cond/branch_3_fun/step_early/pallas_call | solution.py:367
  37.6 0.0 collective-permute-done.3
  37.6 0.0 collective-permute-done.10.refs_2_
  37.6 5.0 %step_late.1 = bf16[2048,512]{1,0:T(8,128)(2,1)} custom-call(s32[16,32]{1,0:T(8,128)S(1)} %convert_convert_fusion.notes_next.notes, s32[3,33]{1,0:T(4,128)S(1)} %get-tuple-element.391.table, s32[1]{0:T(128)} %pick_size.1.refs_0_, bf16[1552,128]{1,0:T(8,128)(2,1)S(1)} %collective-permute-done.8.refs_1_, ...), custom_call_target="tpu_custom_call", output_to_operand_aliasing={{}: (16, {})} | custom-call | flops 536870912 | bytes 4194304 | tf_op jit(solution)/shard_map/step_late/pallas_call | solution.py:367
  (11 shorter events, 0.0 us)
Async XLA Ops:
  0.0 5.2 %copy-start = (bf16[2048,512]{1,0:T(8,128)(2,1)S(1)}, bf16[2048,512]{1,0:T(8,128)(2,1)}, u32[]{:S(2)}) copy-start(bf16[2048,512]{1,0:T(8,128)(2,1)} %f_ref.3) | copy-start | bytes 6291460
  0.0 5.2 %copy-start.4 = (s32[32,1]{0,1:T(1,128)S(1)}, s32[32,1]{0,1:T(1,128)}, u32[]{:S(2)}) copy-start(s32[32,1]{0,1:T(1,128)} %param.14) | copy-start | bytes 388
  0.0 5.2 %copy-start.3 = (s32[32,8]{0,1:T(8,128)S(1)}, s32[32,8]{0,1:T(8,128)}, u32[]{:S(2)}) copy-start(s32[32,8]{0,1:T(8,128)} %param.13) | copy-start | bytes 3076
  0.0 8.3 %copy-start.1 = (bf16[1536,512]{1,0:T(8,128)(2,1)S(1)}, bf16[1536,512]{1,0:T(8,128)(2,1)}, u32[]{:S(2)}) copy-start(bf16[1536,512]{1,0:T(8,128)(2,1)} %refs_1_.1) | copy-start | bytes 4718596
  1.2 17.7 %collective-permute-start.8 = (bf16[1552,128]{1,0:T(8,128)(2,1)S(1)}, bf16[1552,128]{1,0:T(8,128)(2,1)S(1)}, u32[]{:S(2)}, u32[]{:S(2)}) collective-permute-start(bf16[1552,128]{1,0:T(8,128)(2,1)S(1)} %leading_pieces.1), channel_id=1, source_target_pairs={{1,0},{2,1},{3,2},{0,3},{5,4},{6,5},{7,6},{4,7},{9,8},{10,9},{11,1... | collective-permute-start | bytes 1191944 | tf_op jit(solution)/shard_map/ppermute | solution.py:21
  8.3 20.8 %collective-permute-start.12 = (bf16[1536,512]{1,0:T(8,128)(2,1)S(1)}, bf16[1536,512]{1,0:T(8,128)(2,1)S(1)}, u32[]{:S(2)}, u32[]{:S(2)}) collective-permute-start(bf16[1536,512]{1,0:T(8,128)(2,1)S(1)} %copy-done.1), channel_id=1, source_target_pairs={{4,0},{8,4},{12,8},{16,12},{20,16},{24,20},{28,24},{0,28},{5,1},{9... | collective-permute-start | bytes 4718600 | tf_op jit(solution)/shard_map/ppermute | solution.py:21
  12.7 16.2 %collective-permute-start.11 = (bf16[2560,128]{1,0:T(8,128)(2,1)S(1)}, bf16[2560,128]{1,0:T(8,128)(2,1)S(1)}, u32[]{:S(2)}, u32[]{:S(2)}) collective-permute-start(bf16[2560,128]{1,0:T(8,128)(2,1)S(1)} %get-tuple-element.403), channel_id=1, source_target_pairs={{1,0},{2,1},{3,2},{0,3},{5,4},{6,5},{7,6},{4,7},{9,8},{10,9},{11,1... | collective-permute-start | bytes 1966088 | tf_op jit(solution)/shard_map/ppermute | solution.py:21
  18.9 10.2 %copy-start.2 = (f32[2048,512]{1,0:T(8,128)}, f32[2048,512]{1,0:T(8,128)S(1)}, u32[]{:S(2)}) copy-start(f32[2048,512]{1,0:T(8,128)S(1)} %step_first.1.refs_13_) | copy-start | bytes 12582916
  18.9 18.7 %collective-permute-start.10 = (bf16[512,128]{1,0:T(8,128)(2,1)S(1)}, bf16[512,128]{1,0:T(8,128)(2,1)S(1)}, u32[]{:S(2)}, u32[]{:S(2)}) collective-permute-start(bf16[512,128]{1,0:T(8,128)(2,1)S(1)} %get-tuple-element.393), channel_id=1, source_target_pairs={{1,0},{2,1},{3,2},{0,3},{5,4},{6,5},{7,6},{4,7},{9,8},{10,9},{11,1... | collective-permute-start | bytes 393224 | tf_op jit(solution)/shard_map/ppermute | solution.py:21
  22.0 3.7 %collective-permute-start.9 = (s32[8,128]{1,0:T(8,128)S(1)}, s32[8,128]{1,0:T(8,128)S(1)}, u32[]{:S(2)}, u32[]{:S(2)}) collective-permute-start(s32[8,128]{1,0:T(8,128)S(1)} %get-tuple-element.392.one_ref), channel_id=1, source_target_pairs={{2,0},{3,1},{0,2},{1,3},{6,4},{7,5},{4,6},{5,7},{10,8},{11,9},{8,1... | collective-permute-start | bytes 12296 | tf_op jit(solution)/shard_map/ppermute | solution.py:21
  29.1 8.5 %collective-permute-start.3 = (bf16[1024,128]{1,0:T(8,128)(2,1)S(1)}, bf16[1024,128]{1,0:T(8,128)(2,1)}, u32[]{:S(2)}, u32[]{:S(2)}) collective-permute-start(bf16[1024,128]{1,0:T(8,128)(2,1)S(1)} %get-tuple-element.280), channel_id=1, source_target_pairs={{1,0},{2,1},{3,2},{0,3},{5,4},{6,5},{7,6},{4,7},{9,8},{10,9},{11,1... | collective-permute-start | bytes 786440 | tf_op jit(solution)/shard_map/cond/branch_3_fun/ppermute | solution.py:21
where the time goes:
time: 42.8 us; the launch traced here: 42.6 us
  Pallas kernels  23.9 us (56%)
  starting transfers between devices  13.7 us (32%)
  waiting for transfers between devices  4.22 us (10%)
  between operations  0.73 us (2%)
    pallas_call x3, Pallas kernels, step_product(): pl.pallas_call(functools.partial(step_kernel, edge, slots, name, leading,...  15.6 us
    ppermute x6, starting transfers between devices, shifted(): return lax.ppermute(block, axis, route)  13.7 us
    ppermute x6, waiting for transfers between devices, shifted(): return lax.ppermute(block, axis, route)  4.22 us
    pallas_call x1, Pallas kernels, packed_pieces(): pl.pallas_call(functools.partial(pack_kernel, edge, slots), in_specs=[SME...  3.07 us
    pallas_call x1, Pallas kernels, read_notes(): pl.pallas_call(functools.partial(read_kernel, slots), in_specs=[SMEM, SME...  1.82 us
    pallas_call x1, Pallas kernels, cut_pieces(): pl.pallas_call(functools.partial(cut_kernel, rows), in_specs=[ANY], out_s...  1.51 us
    pallas_call x1, Pallas kernels, leading_pieces(): pl.pallas_call(leading_kernel, grid=(1,), in_specs=[pl.BlockSpec((rows *...  1.19 us
  transfers between devices with their start and end apart: 6, of which 3 were waited for; matrix products, arithmetic and copies ran while one was open for 0% of the time, Pallas kernels for 42%

commit v1 on v0

--- a/solution.py
+++ b/solution.py
@@ -149,7 +149,7 @@
     )(f_blocks, cols, counts)
 
 
-def pack_kernel(edge, slots, notes, f_ref, out_ref, extra_ref, table, f_here, packed, sems):
+def pack_kernel(edge, slots, notes, f_ref, out_ref, extra_ref, f_here, packed, sems):
     nrows = notes.shape[1]
     parts = slots // PAIR
     fetched = []
@@ -185,7 +185,6 @@
     ]
     for copy in copies:
         copy.start()
-    write_table(notes, slots, table)
     for copy in copies:
         copy.wait()
 
@@ -197,7 +196,7 @@
     return pl.pallas_call(
         functools.partial(pack_kernel, edge, slots),
         in_specs=[SMEM, ANY],
-        out_specs=[ANY, ANY, SMEM],
+        out_specs=[ANY, ANY],
         scratch_shapes=[
             pltpu.VMEM(f_blocks.shape, f_blocks.dtype),
             pltpu.VMEM(shape, f_blocks.dtype),
@@ -206,7 +205,6 @@
         out_shape=[
             jax.ShapeDtypeStruct(shape, f_blocks.dtype),
             jax.ShapeDtypeStruct((always * edge, PAIR * edge), f_blocks.dtype),
-            table_shape(nrows),
         ],
         cost_estimate=cost(0, 4 * f_blocks.size),
         compiler_params=params(16),
@@ -214,7 +212,7 @@
     )(notes, f_blocks)
 
 
-def cut_kernel(ranges, packed_ref, *refs):
+def cut_kernel(ranges, slots, notes, packed_ref, table, *refs):
     out_refs, sems = refs[: len(ranges)], refs[-1]
     copies = [
         pltpu.make_async_copy(packed_ref.at[pl.ds(low, high - low)], out_ref, sems.at[k])
@@ -222,23 +220,25 @@
     ]
     for copy in copies:
         copy.start()
+    write_table(notes, slots, table)
     for copy in copies:
         copy.wait()
 
 
-def cut_pieces(ranges, packed):
+def cut_pieces(ranges, notes, slots, packed):
     edge = packed.shape[1] // PAIR
     rows = [(low * edge, high * edge) for low, high in ranges]
     return pl.pallas_call(
-        functools.partial(cut_kernel, rows),
-        in_specs=[ANY],
-        out_specs=[ANY] * (2 * len(rows)),
+        functools.partial(cut_kernel, rows, slots),
+        in_specs=[SMEM, ANY],
+        out_specs=[SMEM] + [ANY] * (2 * len(rows)),
         scratch_shapes=[pltpu.SemaphoreType.DMA((len(rows),))],
-        out_shape=[jax.ShapeDtypeStruct((high - low, packed.shape[1]), packed.dtype) for low, high in rows] * 2,
+        out_shape=[table_shape(notes.shape[1])]
+        + [jax.ShapeDtypeStruct((high - low, packed.shape[1]), packed.dtype) for low, high in rows] * 2,
         cost_estimate=cost(0, 4 * sum(high - low for low, high in rows) * packed.shape[1]),
         compiler_params=params(2),
         name="cut_pieces",
-    )(packed)
+    )(notes, packed)
 
 
 def row_product(notes, table, slots, edge, row, held, p_ref):
@@ -405,15 +405,16 @@
     leading = (groups - groups // 4) * GROUP
     others = nrows * (slots // PAIR - 1)
     unit = others // 24
-    always = 10 * unit
+    always = 19 * unit // 2
     ends = [always + k * unit for k in (1, 2, 3, 4, 5, 6, 8)] + [others]
 
     lead = shifted(leading_pieces(leading, f_blocks, cols, counts), "col", -1)
     notes = jnp.concatenate([cols, jnp.broadcast_to(counts, (slots, nrows))], axis=0)
-    packed, extra, table = packed_pieces(notes, slots, always, f_blocks)
+    packed, extra = packed_pieces(notes, slots, always, f_blocks)
     p_second, packed = lax.optimization_barrier((p_matrix, packed))
     p_second = shifted(p_second, "row", -1)
-    rests = cut_pieces([(nrows + always, nrows + end) for end in ends] + [(leading, nrows)], packed)
+    ranges = [(nrows + always, nrows + end) for end in ends] + [(leading, nrows)]
+    table, *rests = cut_pieces(ranges, notes, slots, packed)
     rests, later, unused = rests[: len(ends)], rests[len(ends)], rests[len(ends) + 1 : -1]
     extra, *rests = lax.optimization_barrier((extra, *rests))
     extra = shifted(extra, "col", -1)

time: 42.8 us -> 42.5 us (level)
  waiting for transfers between devices: 4.22 us -> 3.04 us
  Pallas kernels: 23.9 us -> 25 us
    pallas_call x1, Pallas kernels: 1.51 us -> 3.18 us  [cut_pieces(): pl.pallas_call(functools.partial(cut_kernel, rows, slots), in_specs=[SMEM...]
    ppermute x6, waiting for transfers between devices: 4.22 us -> 3.04 us  [shifted(): return lax.ppermute(block, axis, route)]
    pallas_call x1, Pallas kernels: 3.07 us -> 2.24 us  [packed_pieces(): pl.pallas_call(functools.partial(pack_kernel, edge, slots), in_specs=[SME...]
  transfers between devices with their start and end apart: 6 -> 6, of which waited for: 3 -> 2; matrix products, arithmetic and copies ran while one was open for 0% -> 0% of each run, Pallas kernels for 42% -> 42%
where the time goes in v1:
time: 42.5 us
  Pallas kernels  25 us (59%)
  starting transfers between devices  13.5 us (32%)
  waiting for transfers between devices  3.04 us (7%)
  between operations  0.79 us (2%)
    pallas_call x3, Pallas kernels, step_product(): pl.pallas_call(functools.partial(step_kernel, edge, slots, name, leading,...  15.9 us
    ppermute x6, starting transfers between devices, shifted(): return lax.ppermute(block, axis, route)  13.5 us
    pallas_call x1, Pallas kernels, cut_pieces(): pl.pallas_call(functools.partial(cut_kernel, rows, slots), in_specs=[SMEM...  3.18 us
    ppermute x6, waiting for transfers between devices, shifted(): return lax.ppermute(block, axis, route)  3.04 us
    pallas_call x1, Pallas kernels, packed_pieces(): pl.pallas_call(functools.partial(pack_kernel, edge, slots), in_specs=[SME...  2.24 us
    pallas_call x1, Pallas kernels, read_notes(): pl.pallas_call(functools.partial(read_kernel, slots), in_specs=[SMEM, SME...  1.82 us
    pallas_call x1, Pallas kernels, leading_pieces(): pl.pallas_call(leading_kernel, grid=(1,), in_specs=[pl.BlockSpec((rows *...  1.19 us
  transfers between devices with their start and end apart: 6, of which 2 were waited for; matrix products, arithmetic and copies ran while one was open for 0% of the time, Pallas kernels for 42%

profile of v1, /device:TPU:0, one launch (start us, length us, event | category | flops | bytes accessed | tf_op | source)
XLA Modules:
  0.0 42.5 jit_solution(3746786837247795298)
XLA Ops:
  0.0 1.2 %leading_pieces.1 = bf16[1552,128]{1,0:T(8,128)(2,1)S(1)} custom-call(bf16[2048,512]{1,0:T(8,128)(2,1)} %f_ref.3, s32[8,32]{1,0:T(8,128)} %bitcast.4, s32[1,32]{1,0:T(1,128)} %bitcast.6), custom_call_target="tpu_custom_call" | custom-call | bytes 786432 | tf_op jit(solution)/shard_map/leading_pieces/pallas_call | solution.py:136
  1.2 4.0 %collective-permute-start.8 = (bf16[1552,128]{1,0:T(8,128)(2,1)S(1)}, bf16[1552,128]{1,0:T(8,128)(2,1)S(1)}, u32[]{:S(2)}, u32[]{:S(2)}) collective-permute-start(bf16[1552,128]{1,0:T(8,128)(2,1)S(1)} %leading_pieces.1), channel_id=1, source_target_pairs={{1,0},{2,1},{3,2},{0,3},{5,4},{6,5},{7,6},{4,7},{9,8},{10,9},{11,1... | collective-permute-start | bytes 1191944 | tf_op jit(solution)/shard_map/ppermute | solution.py:21
  5.2 0.0 copy-done.4
  5.2 0.0 copy-done.3
  5.2 0.0 copy-done
  5.2 2.2 %pack_live_pieces.1 = (bf16[8192,128]{1,0:T(8,128)(2,1)S(1)}, bf16[2432,128]{1,0:T(8,128)(2,1)S(1)}) custom-call(s32[16,32]{1,0:T(8,128)S(1)} %pad_add_fusion.notes, bf16[2048,512]{1,0:T(8,128)(2,1)S(1)} %copy-done), custom_call_target="tpu_custom_call" | custom-call | bytes 4194304 | tf_op jit(solution)/shard_map/pack_live_pieces/pallas_call | solution.py:196
  7.4 2.7 %collective-permute-start.12 = (bf16[1536,512]{1,0:T(8,128)(2,1)S(1)}, bf16[1536,512]{1,0:T(8,128)(2,1)S(1)}, u32[]{:S(2)}, u32[]{:S(2)}) collective-permute-start(bf16[1536,512]{1,0:T(8,128)(2,1)S(1)} %copy-done.1), channel_id=1, source_target_pairs={{4,0},{8,4},{12,8},{16,12},{20,16},{24,20},{28,24},{0,28},{5,1},{9... | collective-permute-start | bytes 4718600 | tf_op jit(solution)/shard_map/ppermute | solution.py:21
  10.1 3.2 %cut_pieces.1 = (s32[3,33]{1,0:T(4,128)S(1)}, bf16[256,128]{1,0:T(8,128)(2,1)S(1)}, bf16[512,128]{1,0:T(8,128)(2,1)S(1)}, bf16[768,128]{1,0:T(8,128)(2,1)S(1)}, ...) custom-call(s32[16,32]{1,0:T(8,128)S(1)} %pad_add_fusion.notes, ...), custom_call_target="tpu_custom_call" | custom-call | bytes 5963776 | tf_op jit(solution)/shard_map/cut_pieces/pallas_call | solution.py:231
  13.3 1.0 %collective-permute-start.11 = (bf16[2432,128]{1,0:T(8,128)(2,1)S(1)}, bf16[2432,128]{1,0:T(8,128)(2,1)S(1)}, u32[]{:S(2)}, u32[]{:S(2)}) collective-permute-start(bf16[2432,128]{1,0:T(8,128)(2,1)S(1)} %get-tuple-element.403), channel_id=1, source_target_pairs={{1,0},{2,1},{3,2},{0,3},{5,4},{6,5},{7,6},{4,7},{9,8},{10,9},{11,1... | collective-permute-start | bytes 1867784 | tf_op jit(solution)/shard_map/ppermute | solution.py:21
  14.3 5.3 %step_first.1.refs_13_ = f32[2048,512]{1,0:T(8,128)S(1)} custom-call(s32[16,32]{1,0:T(8,128)S(1)} %pad_add_fusion.notes, s32[3,33]{1,0:T(4,128)S(1)} %get-tuple-element.389.table, bf16[8192,128]{1,0:T(8,128)(2,1)S(1)} %get-tuple-element.387.packed_ref.refs_0_, bf16[1536,512]{1,0:T(8,128)(2,1)S(1)} %copy-done.1), custom_call_target="tpu_custom_call" | custom-call | flops 536870912 | bytes 4194304 | tf_op jit(solution)/shard_map/step_first/pallas_call | solution.py:367
  19.6 0.0 collective-permute-done.8.refs_1_
  19.6 1.2 %collective-permute-start.10 = (bf16[512,128]{1,0:T(8,128)(2,1)S(1)}, bf16[512,128]{1,0:T(8,128)(2,1)S(1)}, u32[]{:S(2)}, u32[]{:S(2)}) collective-permute-start(bf16[512,128]{1,0:T(8,128)(2,1)S(1)} %get-tuple-element.393), channel_id=1, source_target_pairs={{1,0},{2,1},{3,2},{0,3},{5,4},{6,5},{7,6},{4,7},{9,8},{10,9},{11,1... | collective-permute-start | bytes 393224 | tf_op jit(solution)/shard_map/ppermute | solution.py:21
  20.8 1.8 %read_notes.1 = (s32[3,33]{1,0:T(4,128)S(1)}, s32[8,128]{1,0:T(8,128)S(1)}) custom-call(s32[16,32]{1,0:T(8,128)S(1)} %pad_add_fusion.notes, s32[16,32]{1,0:T(8,128)S(1)} %convert_convert_fusion.notes_next.notes), custom_call_target="tpu_custom_call" | custom-call | flops 21474836480 | bytes 4096 | tf_op jit(solution)/shard_map/read_notes/pallas_call | solution.py:91
  22.6 1.5 %collective-permute-start.9 = (s32[8,128]{1,0:T(8,128)S(1)}, s32[8,128]{1,0:T(8,128)S(1)}, u32[]{:S(2)}, u32[]{:S(2)}) collective-permute-start(s32[8,128]{1,0:T(8,128)S(1)} %get-tuple-element.392.one_ref), channel_id=1, source_target_pairs={{2,0},{3,1},{0,2},{1,3},{6,4},{7,5},{4,6},{5,7},{10,8},{11,9},{8,1... | collective-permute-start | bytes 12296 | tf_op jit(solution)/shard_map/ppermute | solution.py:21
  24.2 2.1 %collective-permute-done.9.other_ref = s32[8,128]{1,0:T(8,128)S(1)} collective-permute-done((s32[8,128]{1,0:T(8,128)S(1)}, s32[8,128]{1,0:T(8,128)S(1)}, u32[]{:S(2)}, u32[]{:S(2)}) %collective-permute-start.9) | collective-permute-done | bytes 4128 | tf_op jit(solution)/shard_map/ppermute | solution.py:21
  26.3 0.7 %pick_size.1.refs_0_ = s32[1]{0:T(128)} custom-call(s32[8,128]{1,0:T(8,128)S(1)} %get-tuple-element.392.one_ref, s32[8,128]{1,0:T(8,128)S(1)} %collective-permute-done.9.other_ref), custom_call_target="tpu_custom_call" | custom-call | bytes 4096 | tf_op jit(solution)/shard_map/pick_size/pallas_call | solution.py:112
  27.7 0.9 %collective-permute-done.11.refs_3_ = bf16[2432,128]{1,0:T(8,128)(2,1)S(1)} collective-permute-done((bf16[2432,128]{1,0:T(8,128)(2,1)S(1)}, bf16[2432,128]{1,0:T(8,128)(2,1)S(1)}, u32[]{:S(2)}, u32[]{:S(2)}) %collective-permute-start.11) | collective-permute-done | bytes 622624 | tf_op jit(solution)/shard_map/ppermute | solution.py:21
  28.6 0.0 collective-permute-done.12.refs_12_
  28.6 8.0 %conditional.1 = (bf16[2048,512]{1,0:T(8,128)(2,1)}, bf16[256,128]{1,0:T(8,128)(2,1)S(1)}, bf16[512,128]{1,0:T(8,128)(2,1)}, bf16[768,128]{1,0:T(8,128)(2,1)}, b...) conditional(s32[]{:T(128)} %bitcast.3, ...), branch_computations={%region_0.0_spmd, %region_1.0_spmd, %region_2.0_spmd, %region_3.0_... | conditional | flops 536870912 | bytes 8126576 | solution.py:439
  28.6 3.2 %collective-permute-start.3 = (bf16[1024,128]{1,0:T(8,128)(2,1)S(1)}, bf16[1024,128]{1,0:T(8,128)(2,1)}, u32[]{:S(2)}, u32[]{:S(2)}) collective-permute-start(bf16[1024,128]{1,0:T(8,128)(2,1)S(1)} %get-tuple-element.280), channel_id=1, source_target_pairs={{1,0},{2,1},{3,2},{0,3},{5,4},{6,5},{7,6},{4,7},{9,8},{10,9},{11,1... | collective-permute-start | bytes 786440 | tf_op jit(solution)/shard_map/cond/branch_3_fun/ppermute | solution.py:21
  31.9 4.7 %step_early.11 = bf16[2048,512]{1,0:T(8,128)(2,1)} custom-call(s32[16,32]{1,0:T(8,128)S(1)} %get-tuple-element.271.notes, s32[3,33]{1,0:T(4,128)S(1)} %get-tuple-element.272.table, bf16[1552,128]{1,0:T(8,128)(2,1)S(1)} %get-tuple-element.273.refs_0_, bf16[2432,128]{1,0:T(8,128)(2,1)S(1)} %get-tuple-element.274.refs_1_, ...), custom_call_target="tpu_custom_call" | custom-call | flops 536870912 | bytes 4194304 | tf_op jit(solution)/shard_map/cond/branch_3_fun/step_early/pallas_call | solution.py:367
  36.6 0.0 collective-permute-done.3
  36.6 0.0 collective-permute-done.10.refs_2_
  36.6 5.8 %step_late.1 = bf16[2048,512]{1,0:T(8,128)(2,1)} custom-call(s32[16,32]{1,0:T(8,128)S(1)} %convert_convert_fusion.notes_next.notes, s32[3,33]{1,0:T(4,128)S(1)} %get-tuple-element.391.table, s32[1]{0:T(128)} %pick_size.1.refs_0_, bf16[1552,128]{1,0:T(8,128)(2,1)S(1)} %collective-permute-done.8.refs_1_, ...), custom_call_target="tpu_custom_call", output_to_operand_aliasing={{}: (16, {})} | custom-call | flops 536870912 | bytes 4194304 | tf_op jit(solution)/shard_map/step_late/pallas_call | solution.py:367
  (11 shorter events, 0.0 us)
Async XLA Ops:
  0.0 5.2 %copy-start = (bf16[2048,512]{1,0:T(8,128)(2,1)S(1)}, bf16[2048,512]{1,0:T(8,128)(2,1)}, u32[]{:S(2)}) copy-start(bf16[2048,512]{1,0:T(8,128)(2,1)} %f_ref.3) | copy-start | bytes 6291460
  0.0 5.2 %copy-start.4 = (s32[32,1]{0,1:T(1,128)S(1)}, s32[32,1]{0,1:T(1,128)}, u32[]{:S(2)}) copy-start(s32[32,1]{0,1:T(1,128)} %param.14) | copy-start | bytes 388
  0.0 5.2 %copy-start.3 = (s32[32,8]{0,1:T(8,128)S(1)}, s32[32,8]{0,1:T(8,128)}, u32[]{:S(2)}) copy-start(s32[32,8]{0,1:T(8,128)} %param.13) | copy-start | bytes 3076
  0.0 7.4 %copy-start.1 = (bf16[1536,512]{1,0:T(8,128)(2,1)S(1)}, bf16[1536,512]{1,0:T(8,128)(2,1)}, u32[]{:S(2)}) copy-start(bf16[1536,512]{1,0:T(8,128)(2,1)} %refs_1_.1) | copy-start | bytes 4718596
  1.2 18.4 %collective-permute-start.8 = (bf16[1552,128]{1,0:T(8,128)(2,1)S(1)}, bf16[1552,128]{1,0:T(8,128)(2,1)S(1)}, u32[]{:S(2)}, u32[]{:S(2)}) collective-permute-start(bf16[1552,128]{1,0:T(8,128)(2,1)S(1)} %leading_pieces.1), channel_id=1, source_target_pairs={{1,0},{2,1},{3,2},{0,3},{5,4},{6,5},{7,6},{4,7},{9,8},{10,9},{11,1... | collective-permute-start | bytes 1191944 | tf_op jit(solution)/shard_map/ppermute | solution.py:21
  7.4 21.1 %collective-permute-start.12 = (bf16[1536,512]{1,0:T(8,128)(2,1)S(1)}, bf16[1536,512]{1,0:T(8,128)(2,1)S(1)}, u32[]{:S(2)}, u32[]{:S(2)}) collective-permute-start(bf16[1536,512]{1,0:T(8,128)(2,1)S(1)} %copy-done.1), channel_id=1, source_target_pairs={{4,0},{8,4},{12,8},{16,12},{20,16},{24,20},{28,24},{0,28},{5,1},{9... | collective-permute-start | bytes 4718600 | tf_op jit(solution)/shard_map/ppermute | solution.py:21
  13.3 15.3 %collective-permute-start.11 = (bf16[2432,128]{1,0:T(8,128)(2,1)S(1)}, bf16[2432,128]{1,0:T(8,128)(2,1)S(1)}, u32[]{:S(2)}, u32[]{:S(2)}) collective-permute-start(bf16[2432,128]{1,0:T(8,128)(2,1)S(1)} %get-tuple-element.403), channel_id=1, source_target_pairs={{1,0},{2,1},{3,2},{0,3},{5,4},{6,5},{7,6},{4,7},{9,8},{10,9},{11,1... | collective-permute-start | bytes 1867784 | tf_op jit(solution)/shard_map/ppermute | solution.py:21
  19.6 9.0 %copy-start.2 = (f32[2048,512]{1,0:T(8,128)}, f32[2048,512]{1,0:T(8,128)S(1)}, u32[]{:S(2)}) copy-start(f32[2048,512]{1,0:T(8,128)S(1)} %step_first.1.refs_13_) | copy-start | bytes 12582916
  19.6 17.0 %collective-permute-start.10 = (bf16[512,128]{1,0:T(8,128)(2,1)S(1)}, bf16[512,128]{1,0:T(8,128)(2,1)S(1)}, u32[]{:S(2)}, u32[]{:S(2)}) collective-permute-start(bf16[512,128]{1,0:T(8,128)(2,1)S(1)} %get-tuple-element.393), channel_id=1, source_target_pairs={{1,0},{2,1},{3,2},{0,3},{5,4},{6,5},{7,6},{4,7},{9,8},{10,9},{11,1... | collective-permute-start | bytes 393224 | tf_op jit(solution)/shard_map/ppermute | solution.py:21
  22.6 3.7 %collective-permute-start.9 = (s32[8,128]{1,0:T(8,128)S(1)}, s32[8,128]{1,0:T(8,128)S(1)}, u32[]{:S(2)}, u32[]{:S(2)}) collective-permute-start(s32[8,128]{1,0:T(8,128)S(1)} %get-tuple-element.392.one_ref), channel_id=1, source_target_pairs={{2,0},{3,1},{0,2},{1,3},{6,4},{7,5},{4,6},{5,7},{10,8},{11,9},{8,1... | collective-permute-start | bytes 12296 | tf_op jit(solution)/shard_map/ppermute | solution.py:21
  28.6 8.0 %collective-permute-start.3 = (bf16[1024,128]{1,0:T(8,128)(2,1)S(1)}, bf16[1024,128]{1,0:T(8,128)(2,1)}, u32[]{:S(2)}, u32[]{:S(2)}) collective-permute-start(bf16[1024,128]{1,0:T(8,128)(2,1)S(1)} %get-tuple-element.280), channel_id=1, source_target_pairs={{1,0},{2,1},{3,2},{0,3},{5,4},{6,5},{7,6},{4,7},{9,8},{10,9},{11,1... | collective-permute-start | bytes 786440 | tf_op jit(solution)/shard_map/cond/branch_3_fun/ppermute | solution.py:21
